TPU v7x, 32 devices: a whole 2x2x4 slice. The times are simulated.
32 devices in a mesh: dp: 4 (over y, x), expert: 8 (over z, core).
Axes of the slice: x: 2, y: 2, z: 4, core: 2. Of those that a mesh axis runs over, the one named last changes fastest.
Arguments:
- hidden: bfloat16 [4096, 2, 1024], P(('dp', 'expert')), may hold values from -6 to 6
- routes: int32 [4096, 2], P(('dp', 'expert')), may hold values from 0 to 7, all different within a row; in each aligned block of 128 rows (0 to 127, 128 to 255, ...) at most 64 rows name the same one
- gates: float32 [4096, 2], P(('dp', 'expert')), may hold values from 0.1 to 1
- cotangent: bfloat16 [4096, 7168], P(('dp', 'expert')), may hold values from -1.796875 to 1.796875
- weight: bfloat16 [8, 1024, 7168], P('expert', None, 'dp'), may hold values from -0.0625 to 0.0625
Outputs:
- grad_hidden: bfloat16 [4096, 2, 1024], P(('dp', 'expert'))
- grad_gates: float32 [4096, 2], P(('dp', 'expert'))
- grad_weight: bfloat16 [8, 1024, 7168], P('expert', None, 'dp')
Inputs may be any that keep to these rules, and one draw needn't show every extreme that they name: `routes`: each row names 2 different experts; in each aligned block of 128 rows (the rows of one device) no expert is named by more than 64 rows, a bound that some block reaches.
All inputs are finite; a program needn't handle non-finite values.
Results may differ from a plain program's by a relative error of at most 0.0049.
Values may be sent and summed in bfloat16 or wider, within the bound.
A program may use at most 128 MiB of HBM per device.

v0:
```python
import jax
import jax.numpy as jnp
from jax import lax
from jax.sharding import PartitionSpec as P


def per_device(hidden, routes, gates, cotangent, weight):
    local_tokens, top_count, hidden_width = hidden.shape
    columns = lax.axis_size("expert")
    capacity = min(local_tokens, 2 * local_tokens * top_count // columns)
    slot_count = local_tokens * top_count
    flat_experts = routes.reshape(slot_count)
    one_hot = (flat_experts[:, None] == jnp.arange(columns, dtype=jnp.int32)[None, :]).astype(
        jnp.int32
    )
    earlier = jnp.cumsum(one_hot, axis=0) - one_hot
    position = jnp.sum(earlier * one_hot, axis=1)
    destination = flat_experts * capacity + position
    slot_of = (
        jnp.full((columns * capacity,), slot_count, jnp.int32)
        .at[destination]
        .set(jnp.arange(slot_count, dtype=jnp.int32))
    )
    scaled = (
        (gates[:, :, None] * hidden.astype(jnp.float32))
        .astype(jnp.bfloat16)
        .reshape(slot_count, hidden_width)
    )
    scaled = jnp.concatenate([scaled, jnp.zeros((1, hidden_width), jnp.bfloat16)], axis=0)
    cot_pad = jnp.concatenate([cotangent, jnp.zeros((1, cotangent.shape[1]), jnp.bfloat16)], axis=0)
    send_rows = scaled[slot_of].reshape(columns, capacity, hidden_width)
    send_cot = cot_pad[slot_of // top_count].reshape(columns, capacity, cotangent.shape[1])
    got_rows, got_cot = (
        lax.all_to_all(send_rows, "expert", split_axis=0, concat_axis=0, tiled=True),
        lax.all_to_all(send_cot, "expert", split_axis=0, concat_axis=0, tiled=True),
    )
    cot_quarter = lax.all_to_all(got_cot[None], "dp", split_axis=3, concat_axis=0, tiled=True)
    rows_all = lax.all_gather(got_rows[None], "dp", axis=0, tiled=True)
    matrix = weight[0]
    partial_back = jnp.einsum(
        "bscd,fd->bscf", cot_quarter, matrix, preferred_element_type=jnp.float32
    )
    summed = lax.psum_scatter(partial_back, "dp", scatter_dimension=0, tiled=True)
    grad_matrix = jnp.einsum(
        "bscf,bscd->fd", rows_all, cot_quarter, preferred_element_type=jnp.float32
    )
    returned = lax.all_to_all(summed[0], "expert", split_axis=0, concat_axis=0, tiled=True)
    back = returned.reshape(columns * capacity, hidden_width)[destination]
    grad_hidden = (
        (gates.reshape(slot_count)[:, None] * back)
        .astype(jnp.bfloat16)
        .reshape(local_tokens, top_count, hidden_width)
    )
    grad_gates = jnp.sum(
        hidden.reshape(slot_count, hidden_width).astype(jnp.float32) * back, axis=1
    ).reshape(local_tokens, top_count)
    return (grad_hidden, grad_gates, grad_matrix.astype(jnp.bfloat16)[None])


def solution(mesh):
    placed = (
        P(("dp", "expert"), None, None),
        P(("dp", "expert"), None),
        P(("dp", "expert"), None),
        P(("dp", "expert"), None),
        P("expert", None, "dp"),
    )
    return jax.shard_map(
        per_device,
        mesh=mesh,
        in_specs=placed,
        out_specs=(
            P(("dp", "expert"), None, None),
            P(("dp", "expert"), None),
            P("expert", None, "dp"),
        ),
        check_vma=False,
    )
```

profile of v0, /device:TPU:0, one launch (start us, length us, event | category | flops | bytes accessed | tf_op | source)
XLA Modules:
  0.0 597.0 jit_solution(7855034060548513410)
XLA Ops:
  7.2 0.0 reduce-scatter.4.cloned.1.call-start
  7.2 0.8 copy.24
  8.0 0.1 eq.29
  8.1 0.1 eq.25
  8.3 0.7 broadcast_multiply_fusion
  9.0 0.6 reduce-window.6
  9.5 0.2 slice_reduce_fusion
  9.8 0.1 copy.23
  9.9 0.1 mul.41
  10.1 0.1 fusion.13
  10.2 1.4 scatter_custom_fusion
  11.6 1.7 concatenate.6
  13.3 7.1 %gather_fusion = bf16[512,7168]{1,0:T(8,128)(2,1)} fusion(bf16[129,7168]{1,0:T(8,128)(2,1)S(1)} %concatenate.6, s32[1024]{0:T(1024)S(1)} %get-tuple-element.15), kind=kCustom, calls=%fused_computation | custom fusion | bytes 14682112 | tf_op jit(solution)/shard_map/gather | solution.py:32
  20.3 167.8 %all_to_all.33 = bf16[8,64,7168]{2,1,0:T(8,128)(2,1)} all-to-all(bf16[8,64,7168]{2,1,0:T(8,128)(2,1)} %bitcast.50), channel_id=1, replica_groups=mesh['dp'=4,'expert'=8] {'expert'}, dimensions={0} | all-to-all | bytes 14680064 | tf_op jit(solution)/shard_map/all_to_all | solution.py:35
  188.2 16.5 %copy.26 = bf16[1,8,64,7168]{2,1,0,3:T(8,128)(2,1)} copy(bf16[1,8,64,7168]{3,2,1,0:T(8,128)(2,1)} %bitcast.51) | data formatting | bytes 14680064 | tf_op jit(solution)/shard_map/broadcast_in_dim | solution.py:37
  204.7 14.8 %reshape.124 = bf16[4,2,458752]{2,1,0:T(2,128)(2,1)} reshape(bf16[7168,1,8,64]{3,2,1,0:T(8,128)(2,1)} %bitcast.47) | data formatting | bytes 14680064
  219.5 89.5 %all_to_all.34 = bf16[4,2,458752]{2,1,0:T(2,128)(2,1)} all-to-all(bf16[4,2,458752]{2,1,0:T(2,128)(2,1)} %reshape.124), channel_id=1, replica_groups=mesh['dp'=4,'expert'=8] {'dp'}, dimensions={0} | all-to-all | bytes 14680064 | tf_op jit(solution)/shard_map/all_to_all | solution.py:37
  309.0 14.3 %reshape.125 = bf16[7168,1,8,64]{3,2,1,0:T(8,128)(2,1)} reshape(bf16[4,2,458752]{2,1,0:T(2,128)(2,1)} %all_to_all.34) | data formatting | bytes 14680064
  323.3 15.1 %copy.28 = bf16[1,8,64,4,1792]{4,2,1,3,0:T(8,128)(2,1)} copy(bf16[1,8,64,4,1792]{2,1,4,3,0:T(8,128)(2,1)} %bitcast.48) | data formatting | bytes 14680064 | tf_op jit(solution)/shard_map/all_to_all | solution.py:37
  338.5 13.1 %fusion.2 = f32[4,8,64,1024]{3,2,1,0:T(8,128)} fusion(bf16[1,8,64,4,1792]{4,2,1,3,0:T(8,128)(2,1)} %copy.28, bf16[1,1024,1792]{2,1,0:T(8,128)(2,1)} %param.9), kind=kOutput, calls=%fused_computation.7 | convolution fusion | flops 7516192768 | bytes 19398656 | tf_op jit(solution)/shard_map/bscd,fd->bscf/dot_general | solution.py:40
  351.5 0.0 copy-start
  351.5 0.0 reduce-scatter.4.cloned.1.call-update
  351.6 84.3 %reduce-scatter.4.cloned.1.call-done = f32[1,8,64,1024]{3,2,1,0:T(8,128)} async-done(((f32[4,8,64,1024]{3,2,1,0:T(8,128)}), f32[1,8,64,1024]{3,2,1,0:T(8,128)}) %reduce-scatter.4.cloned.1.call-update) | async-done | bytes 2097168
  435.9 4.6 all-to-all-start.2
  440.5 0.0 all-gather.3.cloned.1.call-start
  440.6 0.0 copy-done
  440.6 0.1 copy.22
  440.7 48.9 %all-to-all-done.2 = f32[8,64,1024]{2,1,0:T(8,128)S(1)} async-done(((f32[8,64,1024]{2,1,0:T(8,128)}), f32[8,64,1024]{2,1,0:T(8,128)S(1)}, u32[]{:S(2)}, u32[]{:S(2)}) %all-to-all-start.2) | async-done | bytes 2097184 | tf_op jit(solution)/shard_map/all_to_all | solution.py:47
  489.6 1.1 gather_fusion.1
  490.7 0.6 gather.13
  491.3 3.0 fusion.10
  494.3 0.2 reshape.81
  494.6 2.1 gather_fusion.2
  496.7 29.7 %all_to_all.35 = bf16[8,64,1024]{2,1,0:T(8,128)(2,1)} all-to-all(bf16[8,64,1024]{2,1,0:T(8,128)(2,1)S(1)} %bitcast.52), channel_id=1, replica_groups=mesh['dp'=4,'expert'=8] {'expert'}, dimensions={0} | all-to-all | bytes 2097152 | tf_op jit(solution)/shard_map/all_to_all | solution.py:34
  526.4 0.0 all-gather.3.cloned.1.call-update
  526.4 0.6 copy.29
  527.0 50.1 %all-gather.3.cloned.1.call-done = bf16[32,64,1024]{2,1,0:T(8,128)(2,1)} async-done(((bf16[8,64,1024]{2,1,0:T(8,128)(2,1)}), bf16[32,64,1024]{2,1,0:T(8,128)(2,1)}) %all-gather.3.cloned.1.call-update) | async-done | bytes 4194320 | tf_op jit(solution)/shard_map/all_gather | solution.py:38
  577.1 13.0 %fusion.7 = bf16[1,1024,1792]{2,1,0:T(8,128)(2,1)} fusion(bf16[4,8,64,1024]{3,2,1,0:T(8,128)(2,1)} %bitcast.57, bf16[1,8,64,4,1792]{4,2,1,3,0:T(8,128)(2,1)} %copy.28), kind=kOutput, calls=%fused_computation.10 | convolution fusion | flops 7518027776 | bytes 15204352 | tf_op jit(solution)/shard_map/bscf,bscd->fd/dot_general | solution.py:44
  (9 shorter events, 0.1 us)
Async XLA Ops:
  7.2 428.7 %reduce-scatter.4.cloned.1.call-start = ((), (), s32[]{:S(2)}) async-start(), calls=%async_computation.6 | async-start | bytes 10485760
  351.5 89.0 %copy-start = (f32[128,2]{0,1:T(2,128)S(1)}, f32[128,2]{0,1:T(2,128)}, u32[]{:S(2)}) copy-start(f32[128,2]{0,1:T(2,128)} %param.7) | copy-start | bytes 3076
  435.9 53.7 %all-to-all-start.2 = ((f32[8,64,1024]{2,1,0:T(8,128)}), f32[8,64,1024]{2,1,0:T(8,128)S(1)}, u32[]{:S(2)}, u32[]{:S(2)}) async-start(f32[8,64,1024]{2,1,0:T(8,128)} %bitcast.53), calls=%async_computation.2 | async-start | bytes 4194304 | tf_op jit(solution)/shard_map/all_to_all | solution.py:47
  440.5 136.6 %all-gather.3.cloned.1.call-start = ((), (), s32[]{:S(2)}) async-start(), calls=%async_computation.5 | async-start | bytes 5242880 | tf_op jit(solution)/shard_map/all_gather | solution.py:38
Sparse Core Ops, SparseCore 0:
  351.7 84.1 reduce-scatter.3
  526.5 50.5 all-gather.2
where the time goes:
time: 598 us; the launch traced here: 597 us
  blocking collectives  287 us (48%)
  waiting for transfers between devices  183 us (31%)
  local copies, waits for them, and re-layouts  77.2 us (13%)
  matrix products  26.1 us (4%)
  between operations  14.1 us (2%)
    all_to_all x1, blocking collectives, per_device(): lax.all_to_all(send_cot, 'expert', split_axis=0, concat_axis=0, tiled=True)  168 us
    all_to_all x1, blocking collectives, per_device(): lax.all_to_all(got_cot[None], 'dp', split_axis=3, concat_axis=0, tiled=True)  89.5 us
    unnamed x3, waiting for transfers between devices  84.4 us
    all_gather x1, waiting for transfers between devices, per_device(): rows_all = lax.all_gather(got_rows[None], 'dp', axis=0, tiled=True)  50.1 us
    all_to_all x1, waiting for transfers between devices, per_device(): lax.all_to_all(summed[0], 'expert', split_axis=0, concat_axis=0, tiled=True)  48.9 us
    unnamed x7, local copies, waits for them, and re-layouts  30.6 us
    all_to_all x1, blocking collectives, per_device(): lax.all_to_all(send_rows, 'expert', split_axis=0, concat_axis=0, tiled=True)  29.7 us
    broadcast_in_dim x1, local copies, waits for them, and re-layouts, per_device(): got_cot[None]  16.5 us
  transfers between devices with their start and end apart: 3, of which 3 were waited for; matrix products, arithmetic and copies ran while one was open for 0% of the time, Pallas kernels for 0%

commit v1 on v0

--- a/solution.py
+++ b/solution.py
@@ -4,7 +4,66 @@
 from jax.sharding import PartitionSpec as P
 
 
-def per_device(hidden, routes, gates, cotangent, weight):
+def slots_of(routes, columns, capacity):
+    tokens, top = routes.shape
+    flat = routes.reshape(tokens * top)
+    one_hot = (flat[:, None] == jnp.arange(columns, dtype=jnp.int32)[None, :]).astype(jnp.int32)
+    earlier = jnp.cumsum(one_hot, axis=0) - one_hot
+    position = jnp.sum(earlier * one_hot, axis=1)
+    return flat * capacity + position
+
+
+def gathered(hidden, routes, gates, cotangent, weight):
+    tokens, top, width = hidden.shape
+    columns, groups = lax.axis_size("expert"), lax.axis_size("dp")
+    capacity = min(tokens, 2 * tokens * top // columns)
+    slots = tokens * top
+    part = cotangent.shape[1] // groups
+    quarters = cotangent.reshape(tokens, groups, part).transpose(1, 0, 2)
+    quarters = lax.all_to_all(quarters, "dp", split_axis=0, concat_axis=0, tiled=True)
+    every = lax.all_gather(quarters, "expert", axis=0, tiled=False)
+
+    destination = slots_of(routes, columns, capacity)
+    slot_of = (
+        jnp.full((columns * capacity,), slots, jnp.int32)
+        .at[destination]
+        .set(jnp.arange(slots, dtype=jnp.int32))
+    )
+    scaled = (
+        (gates[:, :, None] * hidden.astype(jnp.float32)).astype(jnp.bfloat16).reshape(slots, width)
+    )
+    scaled = jnp.concatenate([scaled, jnp.zeros((1, width), jnp.bfloat16)], axis=0)
+    rows = scaled[slot_of].reshape(columns, capacity, width)
+    token_of = (slot_of // top).reshape(columns, capacity)
+    rows = lax.all_to_all(rows, "expert", split_axis=0, concat_axis=0, tiled=True)
+    token_of = lax.all_to_all(token_of, "expert", split_axis=0, concat_axis=0, tiled=True)
+    rows = lax.all_gather(rows, "dp", axis=0, tiled=False)
+    token_of = lax.all_gather(token_of, "dp", axis=0, tiled=False)
+
+    block = jnp.arange(columns)[None, :, None] * groups + jnp.arange(groups)[:, None, None]
+    picked = block * tokens + jnp.minimum(token_of, tokens - 1)
+    cot = every.reshape(columns * groups * tokens, part)[picked.reshape(-1)]
+    matrix = weight[0]
+    partial_back = lax.dot_general(
+        cot, matrix, (((1,), (1,)), ((), ())), preferred_element_type=jnp.float32
+    ).astype(jnp.bfloat16)
+    partial_back = partial_back.reshape(groups, columns, capacity, width)
+    summed = lax.psum_scatter(partial_back, "dp", scatter_dimension=0, tiled=True)
+    grad_matrix = lax.dot_general(
+        rows.reshape(-1, width), cot, (((0,), (0,)), ((), ())), preferred_element_type=jnp.float32
+    )
+    returned = lax.all_to_all(summed[0], "expert", split_axis=0, concat_axis=0, tiled=True)
+    back = returned.reshape(columns * capacity, width)[destination].astype(jnp.float32)
+    grad_hidden = (
+        (gates.reshape(slots)[:, None] * back).astype(jnp.bfloat16).reshape(tokens, top, width)
+    )
+    grad_gates = jnp.sum(
+        hidden.reshape(slots, width).astype(jnp.float32) * back, axis=1
+    ).reshape(tokens, top)
+    return (grad_hidden, grad_gates, grad_matrix.astype(jnp.bfloat16)[None])
+
+
+def dispatched(hidden, routes, gates, cotangent, weight):
     local_tokens, top_count, hidden_width = hidden.shape
     columns = lax.axis_size("expert")
     capacity = min(local_tokens, 2 * local_tokens * top_count // columns)
@@ -57,6 +116,13 @@
     return (grad_hidden, grad_gates, grad_matrix.astype(jnp.bfloat16)[None])
 
 
+def per_device(hidden, routes, gates, cotangent, weight):
+    tokens, top = routes.shape
+    capacity = min(tokens, 2 * tokens * top // lax.axis_size("expert"))
+    form = gathered if tokens <= 2 * capacity else dispatched
+    return form(hidden, routes, gates, cotangent, weight)
+
+
 def solution(mesh):
     placed = (
         P(("dp", "expert"), None, None),

time: 598 us -> 399 us (0.67)
  blocking collectives: 287 us -> 65.1 us
  waiting for transfers between devices: 183 us -> 245 us
  local copies, waits for them, and re-layouts: 77.2 us -> 35.9 us
    all_to_all x3 -> x2, blocking collectives: 287 us -> 57.6 us  [the longest x1 29.7 us: gathered(): lax.all_to_all(rows, 'expert', split_axis=0, concat_axis=0, tiled=True)]
    all_gather x1 -> x2, waiting for transfers between devices: 50.1 us -> 162 us  [the longest x1 112 us: gathered(): every = lax.all_gather(quarters, 'expert', axis=0, tiled=False)]
    unnamed x3 -> x4, waiting for transfers between devices: 84.4 us -> 51.1 us
    unnamed x7 -> x10, local copies, waits for them, and re-layouts: 30.6 us -> 4.75 us
    all_to_all x1 -> x2, waiting for transfers between devices: 48.9 us -> 31.7 us  [the longest x1 26.2 us: gathered(): lax.all_to_all(summed[0], 'expert', split_axis=0, concat_axis=0, tiled=True)]
    broadcast_in_dim x1 -> x0, local copies, waits for them, and re-layouts: 16.5 us -> none  [per_device(): got_cot[None]]
    gather x4 -> x3, local copies, waits for them, and re-layouts: 10.8 us -> 24.9 us  [the longest x1 21.7 us: gathered(): cot = every.reshape(columns * groups * tokens, part)[picked.reshape(-1)]]
    all_to_all x1 -> x2, local copies, waits for them, and re-layouts: 15.1 us -> 3.09 us  [the longest x1 2.42 us: gathered(): lax.all_to_all(quarters, 'dp', split_axis=0, concat_axis=0, tiled=True)]
  transfers between devices with their start and end apart: 3 -> 5, of which waited for: 3 -> 5; matrix products, arithmetic and copies ran while one was open for 0% -> 1% of each run, Pallas kernels for 0% -> 0%
where the time goes in v1:
time: 399 us
  waiting for transfers between devices  245 us (61%)
  blocking collectives  65.1 us (16%)
  local copies, waits for them, and re-layouts  35.9 us (9%)
  matrix products  26.2 us (7%)
  between operations  13.9 us (3%)
  starting transfers between devices  10 us (3%)
    all_gather x1, waiting for transfers between devices, gathered(): every = lax.all_gather(quarters, 'expert', axis=0, tiled=False)  112 us
    unnamed x4, waiting for transfers between devices  51.1 us
    all_gather x1, waiting for transfers between devices, gathered(): rows = lax.all_gather(rows, 'dp', axis=0, tiled=False)  50.1 us
    all_to_all x1, blocking collectives, gathered(): lax.all_to_all(rows, 'expert', split_axis=0, concat_axis=0, tiled=True)  29.7 us
    all_to_all x1, blocking collectives, gathered(): lax.all_to_all(quarters, 'dp', split_axis=0, concat_axis=0, tiled=True)  27.9 us
    all_to_all x1, waiting for transfers between devices, gathered(): lax.all_to_all(summed[0], 'expert', split_axis=0, concat_axis=0, tiled=True)  26.2 us
    gather x1, local copies, waits for them, and re-layouts, gathered(): cot = every.reshape(columns * groups * tokens, part)[picked.reshape(-1)]  21.7 us
    dot_general x1, matrix products, gathered(): lax.dot_general(cot, matrix, (((1,), (1,)), ((), ())), preferred_element_...  13.1 us
  transfers between devices with their start and end apart: 5, of which 5 were waited for; matrix products, arithmetic and copies ran while one was open for 1% of the time, Pallas kernels for 0%

profile of v1, /device:TPU:0, one launch (start us, length us, event | category | flops | bytes accessed | tf_op | source)
XLA Modules:
  0.0 398.7 jit_solution(3642541819108778224)
XLA Ops:
  7.2 0.0 all-gather.6.cloned.1.call-start
  7.2 3.9 copy.28
  11.1 0.0 copy-start.1
  11.1 27.9 %all_to_all.24 = bf16[4,128,1792]{1,2,0:T(8,128)(2,1)S(1)} all-to-all(bf16[4,128,1792]{1,2,0:T(8,128)(2,1)} %bitcast.34), channel_id=1, replica_groups=mesh['dp'=4,'expert'=8] {'dp'}, dimensions={0} | all-to-all | bytes 3670016 | tf_op jit(solution)/shard_map/all_to_all | solution.py:23
  38.9 2.4 copy.29
  41.4 0.0 all-gather.6.cloned.1.call-update
  41.4 0.0 copy-done.1
  41.4 0.1 copy.31
  41.5 0.1 eq.29
  41.7 0.1 eq.25
  41.8 0.6 reduce-window.6
  42.4 0.2 slice_reduce_fusion
  42.7 0.1 copy.30
  42.8 0.1 mul.63
  42.9 0.1 fusion.5
  43.0 1.4 scatter_custom_fusion
  44.5 0.7 all_to_all.16
  45.1 5.0 %all-to-all-start.1 = ((s32[8,1,64]{2,1,0:T(1,128)}), s32[8,1,64]{2,1,0:T(1,128)S(1)}, u32[]{:S(2)}, u32[]{:S(2)}) async-start(s32[8,1,64]{2,1,0:T(1,128)} %all_to_all.16), calls=%async_computation.1 | async-start | bytes 8192 | tf_op jit(solution)/shard_map/all_to_all | solution.py:39
  50.1 0.0 reduce-scatter.4.cloned.1.call-start
  50.2 5.4 %all-to-all-done.1 = s32[8,1,64]{2,1,0:T(1,128)S(1)} async-done(((s32[8,1,64]{2,1,0:T(1,128)}), s32[8,1,64]{2,1,0:T(1,128)S(1)}, u32[]{:S(2)}, u32[]{:S(2)}) %all-to-all-start.1) | async-done | bytes 2080 | tf_op jit(solution)/shard_map/all_to_all | solution.py:39
  55.6 7.5 %all-gather.1 = s32[32,1,64]{2,1,0:T(1,128)S(1)} all-gather(s32[8,1,64]{2,1,0:T(1,128)S(1)} %all-to-all-done.1), channel_id=3, replica_groups=mesh['dp'=4,'expert'=8] {'dp'}, dimensions={0}, use_global_device_ids=true | all-gather | bytes 10240 | tf_op jit(solution)/shard_map/all_gather | solution.py:41
  63.2 0.1 bitcast_add_fusion
  63.3 0.1 reshape.158
  63.4 112.0 %all-gather.6.cloned.1.call-done = bf16[32,128,1792]{2,1,0:T(8,128)(2,1)} async-done(((bf16[4,128,1792]{2,1,0:T(8,128)(2,1)}), bf16[32,128,1792]{2,1,0:T(8,128)(2,1)}) %all-gather.6.cloned.1.call-update) | async-done | bytes 14680080 | tf_op jit(solution)/shard_map/all_gather | solution.py:24
  175.3 21.7 %gather_fusion = bf16[2048,1792]{1,0:T(8,128)(2,1)} fusion(bf16[4096,1792]{1,0:T(8,128)(2,1)} %bitcast.32, s32[2048]{0:T(1024)S(1)} %broadcast_clamp_fusion), kind=kCustom, calls=%fused_computation | custom fusion | bytes 14688256 | tf_op jit(solution)/shard_map/gather | solution.py:45
  197.0 13.1 %convolution_convert_fusion.1 = bf16[2048,1024]{1,0:T(8,128)(2,1)} fusion(bf16[2048,1792]{1,0:T(8,128)(2,1)} %gather_fusion, bf16[1,1024,1792]{2,1,0:T(8,128)(2,1)} %param.9), kind=kOutput, calls=%fused_computation.5 | convolution fusion | flops 7518289920 | bytes 15204352 | tf_op jit(solution)/shard_map/dot_general | solution.py:47
  210.1 0.0 copy-start.2
  210.1 0.0 reduce-scatter.4.cloned.1.call-update
  210.2 51.0 %reduce-scatter.4.cloned.1.call-done = bf16[1,8,64,1024]{3,2,1,0:T(8,128)(2,1)} async-done(((bf16[4,8,64,1024]{3,2,1,0:T(8,128)(2,1)}), bf16[1,8,64,1024]{3,2,1,0:T(8,128)(2,1)}) %reduce-scatter.4.cloned.1.call-update) | async-done | bytes 1048592
  261.2 0.0 copy-start
  261.2 4.7 %all-to-all-start.2 = ((bf16[8,64,1024]{2,1,0:T(8,128)(2,1)}), bf16[8,64,1024]{2,1,0:T(8,128)(2,1)S(1)}, u32[]{:S(2)}, u32[]{:S(2)}) async-start(bf16[8,64,1024]{2,1,0:T(8,128)(2,1)} %bitcast.37), calls=%async_computation.2 | async-start | bytes 2097152 | tf_op jit(solution)/shard_map/all_to_all | solution.py:55
  265.9 0.2 all-gather.8.cloned.1.call-start
  266.2 0.0 copy-done.2
  266.2 0.1 copy.27
  266.3 26.2 %all-to-all-done.2 = bf16[8,64,1024]{2,1,0:T(8,128)(2,1)S(1)} async-done(((bf16[8,64,1024]{2,1,0:T(8,128)(2,1)}), bf16[8,64,1024]{2,1,0:T(8,128)(2,1)S(1)}, u32[]{:S(2)}, u32[]{:S(2)}) %all-to-all-start.2) | async-done | bytes 1048608 | tf_op jit(solution)/shard_map/all_to_all | solution.py:55
  292.5 1.2 gather_fusion.1
  293.7 0.7 reshape.164
  294.4 0.0 copy-done
  294.4 2.0 fusion.2
  296.4 0.2 reshape.161
  296.6 2.1 gather_fusion.2
  298.7 29.7 %all_to_all.25 = bf16[8,64,1024]{2,1,0:T(8,128)(2,1)} all-to-all(bf16[8,64,1024]{2,1,0:T(8,128)(2,1)S(1)} %bitcast.35), channel_id=1, replica_groups=mesh['dp'=4,'expert'=8] {'expert'}, dimensions={0} | all-to-all | bytes 2097152 | tf_op jit(solution)/shard_map/all_to_all | solution.py:38
  328.4 0.0 all-gather.8.cloned.1.call-update
  328.4 0.6 copy.33
  329.0 50.1 %all-gather.8.cloned.1.call-done = bf16[32,64,1024]{2,1,0:T(8,128)(2,1)} async-done(((bf16[8,64,1024]{2,1,0:T(8,128)(2,1)}), bf16[32,64,1024]{2,1,0:T(8,128)(2,1)}) %all-gather.8.cloned.1.call-update) | async-done | bytes 4194320 | tf_op jit(solution)/shard_map/all_gather | solution.py:40
  379.2 13.0 %fusion.1 = bf16[1,1024,1792]{2,1,0:T(8,128)(2,1)} fusion(bf16[2048,1024]{1,0:T(8,128)(2,1)} %bitcast.43, bf16[2048,1792]{1,0:T(8,128)(2,1)} %gather_fusion), kind=kOutput, calls=%fused_computation.7 | convolution fusion | flops 7518027776 | bytes 15204352 | tf_op jit(solution)/shard_map/dot_general | solution.py:52
  (15 shorter events, 0.2 us)
Async XLA Ops:
  7.2 168.2 %all-gather.6.cloned.1.call-start = ((), (), s32[]{:S(2)}) async-start(), calls=%async_computation.5 | async-start | bytes 16515072 | tf_op jit(solution)/shard_map/all_gather | solution.py:24
  11.1 30.3 %copy-start.1 = (s32[128,2]{0,1:T(2,128)S(1)}, s32[128,2]{0,1:T(2,128)}, u32[]{:S(2)}) copy-start(s32[128,2]{0,1:T(2,128)} %param.6) | copy-start | bytes 3076
  45.1 10.5 %all-to-all-start.1 = ((s32[8,1,64]{2,1,0:T(1,128)}), s32[8,1,64]{2,1,0:T(1,128)S(1)}, u32[]{:S(2)}, u32[]{:S(2)}) async-start(s32[8,1,64]{2,1,0:T(1,128)} %all_to_all.16), calls=%async_computation.1 | async-start | bytes 8192 | tf_op jit(solution)/shard_map/all_to_all | solution.py:39
  50.1 211.1 %reduce-scatter.4.cloned.1.call-start = ((), (), s32[]{:S(2)}) async-start(), calls=%async_computation.7 | async-start | bytes 5242880
  210.1 56.0 %copy-start.2 = (f32[128,2]{0,1:T(2,128)S(1)}, f32[128,2]{0,1:T(2,128)}, u32[]{:S(2)}) copy-start(f32[128,2]{0,1:T(2,128)} %param.7) | copy-start | bytes 3076
  261.2 33.2 %copy-start = (bf16[128,2,1024]{2,1,0:T(2,128)(2,1)S(1)}, bf16[128,2,1024]{2,1,0:T(2,128)(2,1)}, u32[]{:S(2)}) copy-start(bf16[128,2,1024]{2,1,0:T(2,128)(2,1)} %param.5) | copy-start | bytes 1572868
  261.2 31.3 %all-to-all-start.2 = ((bf16[8,64,1024]{2,1,0:T(8,128)(2,1)}), bf16[8,64,1024]{2,1,0:T(8,128)(2,1)S(1)}, u32[]{:S(2)}, u32[]{:S(2)}) async-start(bf16[8,64,1024]{2,1,0:T(8,128)(2,1)} %bitcast.37), calls=%async_computation.2 | async-start | bytes 2097152 | tf_op jit(solution)/shard_map/all_to_all | solution.py:55
  265.9 113.2 %all-gather.8.cloned.1.call-start = ((), (), s32[]{:S(2)}) async-start(), calls=%async_computation.6 | async-start | bytes 5242880 | tf_op jit(solution)/shard_map/all_gather | solution.py:40
Sparse Core Ops, SparseCore 0:
  41.5 133.7 all-gather.5
  210.3 50.8 reduce-scatter.3
  328.5 50.5 all-gather.7

commit v2 on v1

--- a/solution.py
+++ b/solution.py
@@ -1,16 +1,135 @@
+import functools
+
 import jax
 import jax.numpy as jnp
 from jax import lax
+from jax.experimental import pallas as pl
+from jax.experimental.pallas import tpu as pltpu
 from jax.sharding import PartitionSpec as P
 
-
-def slots_of(routes, columns, capacity):
-    tokens, top = routes.shape
-    flat = routes.reshape(tokens * top)
-    one_hot = (flat[:, None] == jnp.arange(columns, dtype=jnp.int32)[None, :]).astype(jnp.int32)
-    earlier = jnp.cumsum(one_hot, axis=0) - one_hot
-    position = jnp.sum(earlier * one_hot, axis=1)
-    return flat * capacity + position
+MESH = pl.DeviceIdType.MESH
+
+
+def exchange(groups, columns, quarters, packed, every, rows, local_sem, dp_send, dp_recv, side_send,
+             up_send, down_send, line_recv, side_recv, rows_send, rows_recv, pass_send, pass_recv):
+    group, mine = lax.axis_index("dp"), lax.axis_index("expert")
+    depth = columns // 2
+    level, core = mine // 2, lax.rem(mine, 2)
+
+    def other(index, step, size):
+        return lax.rem(index + step, size)
+
+    barrier = pltpu.get_barrier_semaphore()
+    for step in range(1, groups):
+        pl.semaphore_signal(barrier, inc=1, device_id=(other(group, step, groups), mine), device_id_type=MESH)
+    for step in range(1, columns):
+        pl.semaphore_signal(barrier, inc=1, device_id=(group, other(mine, step, columns)), device_id_type=MESH)
+    pl.semaphore_wait(barrier, groups + columns - 2)
+
+    def remote(source, target, send, recv, device):
+        return pltpu.make_async_remote_copy(
+            src_ref=source, dst_ref=target, send_sem=send, recv_sem=recv, device_id=device, device_id_type=MESH
+        )
+
+    def to_group(step):
+        there = other(group, step, groups)
+        return remote(quarters.at[there], every.at[group, mine], dp_send.at[step], dp_recv.at[step], (there, mine))
+
+    def to_expert(step):
+        there = other(mine, step, columns)
+        return remote(packed.at[there], rows.at[group, mine], rows_send.at[step], rows_recv.at[step], (group, there))
+
+    def chunk(start, step):
+        source = lax.rem(group - step + groups, groups)
+        place = every.at[source, start * 2 + core]
+        return place, source
+
+    def on_line(start, step, move, first=False):
+        place, source = chunk(start, step)
+        send = (up_send if move > 0 else down_send).at[start, step]
+        origin = quarters.at[group] if first else place
+        return remote(origin, place, send, line_recv.at[start, step], (group, (level + move) * 2 + core))
+
+    def to_side(start, step, first=False):
+        place, source = chunk(start, step)
+        origin = quarters.at[group] if first else place
+        return remote(origin, place, side_send.at[start, step], side_recv.at[start, step], (group, level * 2 + 1 - core))
+
+    def pass_on(step, hop):
+        start = lax.rem(mine - step + columns, columns)
+        place = rows.at[group, start]
+        origin = packed.at[mine] if step == 0 else place
+        return remote(origin, place, pass_send.at[hop, step], pass_recv.at[hop, step], (other(group, hop, groups), mine))
+
+    own_cot = pltpu.make_async_copy(quarters.at[group], every.at[group, mine], local_sem.at[0])
+    own_rows = pltpu.make_async_copy(packed.at[mine], rows.at[group, mine], local_sem.at[1])
+
+    for step in range(1, groups):
+        to_group(step).start()
+    for step in range(groups):
+        if step:
+            to_group(step).wait_recv()
+        first = step == 0
+
+        @pl.when(level < depth - 1)
+        def _():
+            on_line(level, step, 1, first).start()
+
+        @pl.when(level > 0)
+        def _():
+            on_line(level, step, -1, first).start()
+
+        to_side(level, step, first).start()
+        if first:
+            own_cot.start()
+            own_rows.start()
+            for peer in range(1, columns):
+                to_expert(peer).start()
+            for hop in range(1, groups):
+                pass_on(0, hop).start()
+    for distance in range(1, depth):
+        for step in range(groups):
+            for move in (1, -1):
+                start = level - move * distance
+                inside = (start >= 0) & (start < depth)
+                onward = (level < depth - 1) if move > 0 else (level > 0)
+
+                @pl.when(inside)
+                def _():
+                    on_line(start, step, move).wait_recv()
+                    to_side(start, step).start()
+
+                @pl.when(inside & onward)
+                def _():
+                    on_line(start, step, move).start()
+
+        if distance == 1:
+            for peer in range(1, columns):
+                to_expert(peer).wait_recv()
+                for hop in range(1, groups):
+                    pass_on(peer, hop).start()
+
+    own_cot.wait()
+    own_rows.wait()
+    for step in range(1, groups):
+        to_group(step).wait_send()
+    for peer in range(1, columns):
+        to_expert(peer).wait_send()
+    for step in range(groups):
+        for start in range(depth):
+            to_side(start, step).wait()
+
+            @pl.when((level < depth - 1) & (level >= start))
+            def _():
+                on_line(start, step, 1).wait_send()
+
+            @pl.when((level > 0) & (level <= start))
+            def _():
+                on_line(start, step, -1).wait_send()
+
+    for hop in range(1, groups):
+        for peer in range(columns):
+            pass_on(peer, hop).wait()
 
 
 def gathered(hidden, routes, gates, cotangent, weight):
@@ -20,40 +139,72 @@
     slots = tokens * top
     part = cotangent.shape[1] // groups
     quarters = cotangent.reshape(tokens, groups, part).transpose(1, 0, 2)
-    quarters = lax.all_to_all(quarters, "dp", split_axis=0, concat_axis=0, tiled=True)
-    every = lax.all_gather(quarters, "expert", axis=0, tiled=False)
-
-    destination = slots_of(routes, columns, capacity)
-    slot_of = (
-        jnp.full((columns * capacity,), slots, jnp.int32)
-        .at[destination]
-        .set(jnp.arange(slots, dtype=jnp.int32))
+
+    flat = routes.reshape(slots)
+    named = (flat[:, None] == jnp.arange(columns, dtype=jnp.int32)[None, :]).astype(jnp.int32)
+    position = jnp.sum((jnp.cumsum(named, axis=0) - named) * named, axis=1)
+    destination = flat * capacity + position
+    places = jnp.arange(columns * capacity, dtype=jnp.int32)
+    choose = (places[:, None] == destination[None, :]).astype(jnp.bfloat16)
+    by_slot = destination.reshape(tokens, top)
+    token_of = sum(
+        (places[:, None] == by_slot[None, :, slot]).astype(jnp.bfloat16) for slot in range(top)
     )
     scaled = (
         (gates[:, :, None] * hidden.astype(jnp.float32)).astype(jnp.bfloat16).reshape(slots, width)
     )
-    scaled = jnp.concatenate([scaled, jnp.zeros((1, width), jnp.bfloat16)], axis=0)
-    rows = scaled[slot_of].reshape(columns, capacity, width)
-    token_of = (slot_of // top).reshape(columns, capacity)
-    rows = lax.all_to_all(rows, "expert", split_axis=0, concat_axis=0, tiled=True)
-    token_of = lax.all_to_all(token_of, "expert", split_axis=0, concat_axis=0, tiled=True)
-    rows = lax.all_gather(rows, "dp", axis=0, tiled=False)
-    token_of = lax.all_gather(token_of, "dp", axis=0, tiled=False)
-
-    block = jnp.arange(columns)[None, :, None] * groups + jnp.arange(groups)[:, None, None]
-    picked = block * tokens + jnp.minimum(token_of, tokens - 1)
-    cot = every.reshape(columns * groups * tokens, part)[picked.reshape(-1)]
-    matrix = weight[0]
+    packed = jnp.concatenate(
+        [jnp.dot(choose, scaled, preferred_element_type=jnp.float32).astype(jnp.bfloat16), token_of], axis=1
+    ).reshape(columns, capacity, width + tokens)
+
+    sems = pltpu.SemaphoreType.DMA
+    depth = columns // 2
+    every, rows = pl.pallas_call(
+        functools.partial(exchange, groups, columns),
+        out_shape=(
+            jax.ShapeDtypeStruct((groups, columns, tokens, part), jnp.bfloat16),
+            jax.ShapeDtypeStruct((groups, columns, capacity, width + tokens), jnp.bfloat16),
+        ),
+        in_specs=[pl.BlockSpec(memory_space=pl.ANY)] * 2,
+        out_specs=[pl.BlockSpec(memory_space=pl.ANY)] * 2,
+        scratch_shapes=[
+            sems((2,)),
+            sems((groups,)),
+            sems((groups,)),
+            sems((depth, groups)),
+            sems((depth, groups)),
+            sems((depth, groups)),
+            sems((depth, groups)),
+            sems((depth, groups)),
+            sems((columns,)),
+            sems((columns,)),
+            sems((groups, columns)),
+            sems((groups, columns)),
+        ],
+        compiler_params=pltpu.CompilerParams(collective_id=0, has_side_effects=True),
+        name="exchange",
+    )(quarters, packed)
+
+    blocks = groups * columns
+    sent, token_of = rows[..., :width], rows[..., width:]
+    cot = lax.dot_general(
+        token_of.reshape(blocks, capacity, tokens),
+        every.reshape(blocks, tokens, part),
+        (((2,), (1,)), ((0,), (0,))),
+        preferred_element_type=jnp.float32,
+    ).astype(jnp.bfloat16).reshape(blocks * capacity, part)
     partial_back = lax.dot_general(
-        cot, matrix, (((1,), (1,)), ((), ())), preferred_element_type=jnp.float32
+        cot, weight[0], (((1,), (1,)), ((), ())), preferred_element_type=jnp.float32
     ).astype(jnp.bfloat16)
     partial_back = partial_back.reshape(groups, columns, capacity, width)
     summed = lax.psum_scatter(partial_back, "dp", scatter_dimension=0, tiled=True)
     grad_matrix = lax.dot_general(
-        rows.reshape(-1, width), cot, (((0,), (0,)), ((), ())), preferred_element_type=jnp.float32
+        sent.reshape(blocks * capacity, width), cot, (((0,), (0,)), ((), ())), preferred_element_type=jnp.float32
     )
     returned = lax.all_to_all(summed[0], "expert", split_axis=0, concat_axis=0, tiled=True)
-    back = returned.reshape(columns * capacity, width)[destination].astype(jnp.float32)
+    back = lax.dot_general(
+        choose, returned.reshape(columns * capacity, width), (((0,), (0,)), ((), ())), preferred_element_type=jnp.float32
+    )
     grad_hidden = (
         (gates.reshape(slots)[:, None] * back).astype(jnp.bfloat16).reshape(tokens, top, width)
     )

time: 399 us -> 278 us (0.70)
  waiting for transfers between devices: 245 us -> 60.2 us
  Pallas kernels: 0 us -> 147 us
  blocking collectives: 65.1 us -> 0 us
  local copies, waits for them, and re-layouts: 35.9 us -> 16.4 us
  starting transfers between devices: 10 us -> 4.65 us
  matrix products: 26.2 us -> 31 us
    all_gather x2 -> x0, waiting for transfers between devices: 162 us -> none  [the longest x1 112 us: gathered(): every = lax.all_gather(quarters, 'expert', axis=0, tiled=False)]
    pallas_call x0 -> x1, Pallas kernels: none -> 147 us  [gathered(): pl.pallas_call(functools.partial(exchange, groups, columns), out_shape=(j...]
    all_to_all x2 -> x0, blocking collectives: 57.6 us -> none  [the longest x1 29.7 us: gathered(): lax.all_to_all(rows, 'expert', split_axis=0, concat_axis=0, tiled=True)]
    gather x3 -> x0, local copies, waits for them, and re-layouts: 24.9 us -> none  [the longest x1 21.7 us: gathered(): cot = every.reshape(columns * groups * tokens, part)[picked.reshape(-1)]]
    all_to_all x1, waiting for transfers between devices: 26.2 us -> 8.19 us  [gathered(): lax.all_to_all(summed[0], 'expert', split_axis=0, concat_axis=0, tiled=True)]
    all_gather x1 -> x0, blocking collectives: 7.52 us -> none  [gathered(): token_of = lax.all_gather(token_of, 'dp', axis=0, tiled=False)]
    slice x1 -> x3, local copies, waits for them, and re-layouts: 0.21 us -> 6.33 us  [the longest x2 6.12 us: gathered(): sent, token_of = (rows[..., :width], rows[..., width:])]
    all_to_all x1 -> x0, waiting for transfers between devices: 5.45 us -> none  [gathered(): lax.all_to_all(token_of, 'expert', split_axis=0, concat_axis=0, tiled=True)]
  transfers between devices with their start and end apart: 5 -> 2, of which waited for: 5 -> 2; matrix products, arithmetic and copies ran while one was open for 1% -> 7% of each run, Pallas kernels for 0% -> 0%
where the time goes in v2:
time: 278 us
  Pallas kernels  147 us (53%)
  waiting for transfers between devices  60.2 us (22%)
  matrix products  31 us (11%)
  local copies, waits for them, and re-layouts  16.4 us (6%)
  between operations  14.2 us (5%)
  starting transfers between devices  4.65 us (2%)
  other arithmetic  4.15 us (1%)
    pallas_call x1, Pallas kernels, gathered(): pl.pallas_call(functools.partial(exchange, groups, columns), out_shape=(j...  147 us
    unnamed x2, waiting for transfers between devices  52 us
    dot_general x1, matrix products, gathered(): lax.dot_general(sent.reshape(blocks * capacity, width), cot, (((0,), (0,)...  13.1 us
    dot_general x1, matrix products, gathered(): lax.dot_general(cot, weight[0], (((1,), (1,)), ((), ())), preferred_eleme...  9.47 us
    all_to_all x1, waiting for transfers between devices, gathered(): lax.all_to_all(summed[0], 'expert', split_axis=0, concat_axis=0, tiled=True)  8.19 us
    dot_general x1, matrix products, gathered(): lax.dot_general(token_of.reshape(blocks, capacity, tokens), every.reshape...  7.45 us
    slice x2, local copies, waits for them, and re-layouts, gathered(): sent, token_of = (rows[..., :width], rows[..., width:])  6.12 us
  transfers between devices with their start and end apart: 2, of which 2 were waited for; matrix products, arithmetic and copies ran while one was open for 7% of the time, Pallas kernels for 0%

profile of v2, /device:TPU:0, one launch (start us, length us, event | category | flops | bytes accessed | tf_op | source)
XLA Modules:
  0.0 277.8 jit_solution(14346596487976663764)
XLA Ops:
  7.2 0.0 reduce-scatter.4.cloned.1.call-start
  7.2 0.8 copy.37
  8.0 0.1 eq.70
  8.1 0.1 reshape.76
  8.3 0.6 reduce-window.6
  8.9 0.2 slice_reduce_fusion
  9.1 0.1 fusion.9
  9.2 0.1 reduce_sum.21
  9.4 0.1 copy.42
  9.5 0.7 multiply_add_fusion
  10.2 0.8 copy.36
  10.9 1.5 multiply_convert_fusion.1
  12.5 0.2 reshape.79
  12.7 3.3 %copy.39 = bf16[128,7168]{0,1:T(8,128)(2,1)S(1)} copy(bf16[128,7168]{1,0:T(8,128)(2,1)} %param.8) | data formatting | bytes 3670016 | tf_op args[3]
  16.0 2.4 copy.40
  18.4 0.1 fusion.7
  18.5 0.4 convolution_convert_fusion.3
  18.9 1.1 pad_maximum_fusion
  20.1 147.3 %exchange.1 = (bf16[4,8,128,1792]{3,2,1,0:T(8,128)(2,1)}, bf16[4,8,64,1152]{3,2,1,0:T(8,128)(2,1)}) custom-call(bf16[4,128,1792]{2,1,0:T(8,128)(2,1)} %bitcast.39, bf16[8,64,1152]{2,1,0:T(8,128)(2,1)} %bitcast.40), custom_call_target="tpu_custom_call" | custom-call | tf_op jit(solution)/shard_map/exchange/pallas_call | solution.py:162
  167.4 1.1 slice.22
  168.4 0.0 copy-start.2
  168.4 7.4 %convolution_convert_fusion = bf16[32,64,1792]{2,1,0:T(8,128)(2,1)S(1)} fusion(bf16[32,64,128]{2,1,0:T(8,128)(2,1)S(1)} %bitcast.44, bf16[32,128,1792]{2,1,0:T(8,128)(2,1)} %bitcast.35), kind=kOutput, calls=%fused_computation | convolution fusion | flops 943194112 | bytes 22544384 | tf_op jit(solution)/shard_map/dot_general | solution.py:190
  175.9 0.0 copy-start
  175.9 0.0 copy-done.2
  175.9 9.5 %convolution_convert_fusion.2 = bf16[2048,1024]{1,0:T(8,128)(2,1)} fusion(bf16[2048,1792]{1,0:T(8,128)(2,1)S(1)} %bitcast.36, bf16[1,1024,1792]{2,1,0:T(8,128)(2,1)S(1)} %copy-done.2), kind=kOutput, calls=%fused_computation.2 | convolution fusion | flops 7518289920 | bytes 15204352 | tf_op jit(solution)/shard_map/dot_general | solution.py:196
  185.4 0.0 copy-done
  185.4 0.0 reduce-scatter.4.cloned.1.call-update
  185.4 52.0 %reduce-scatter.4.cloned.1.call-done = bf16[1,8,64,1024]{3,2,1,0:T(8,128)(2,1)} async-done(((bf16[4,8,64,1024]{3,2,1,0:T(8,128)(2,1)}), bf16[1,8,64,1024]{3,2,1,0:T(8,128)(2,1)}) %reduce-scatter.4.cloned.1.call-update) | async-done | bytes 1048592
  237.4 4.6 %all-to-all-start = ((bf16[8,64,1024]{2,1,0:T(8,128)(2,1)}), bf16[8,64,1024]{2,1,0:T(8,128)(2,1)S(1)}, u32[]{:S(2)}, u32[]{:S(2)}) async-start(bf16[8,64,1024]{2,1,0:T(8,128)(2,1)} %bitcast.45), calls=%async_computation | async-start | bytes 2097152 | tf_op jit(solution)/shard_map/all_to_all | solution.py:204
  242.0 0.0 copy-start.1
  242.0 5.0 %slice.23 = bf16[4,8,64,1024]{3,2,1,0:T(8,128)(2,1)} slice(bf16[4,8,64,1152]{3,2,1,0:T(8,128)(2,1)} %get-tuple-element.5), slice={[0:4], [0:8], [0:64], [0:1024]} | slice | bytes 8388608 | tf_op jit(solution)/shard_map/slice | solution.py:189
  247.1 0.1 mul.39
  247.2 0.0 copy-done.1
  247.2 0.1 reshape.89
  247.4 13.1 %fusion.1 = bf16[1,1024,1792]{2,1,0:T(8,128)(2,1)} fusion(bf16[2048,1024]{1,0:T(8,128)(2,1)} %bitcast.42, bf16[2048,1792]{1,0:T(8,128)(2,1)} %bitcast.37), kind=kOutput, calls=%fused_computation.4 | convolution fusion | flops 7518027776 | bytes 15204352 | tf_op jit(solution)/shard_map/dot_general | solution.py:201
  260.4 8.2 %all-to-all-done = bf16[8,64,1024]{2,1,0:T(8,128)(2,1)S(1)} async-done(((bf16[8,64,1024]{2,1,0:T(8,128)(2,1)}), bf16[8,64,1024]{2,1,0:T(8,128)(2,1)S(1)}, u32[]{:S(2)}, u32[]{:S(2)}) %all-to-all-start) | async-done | bytes 1048608 | tf_op jit(solution)/shard_map/all_to_all | solution.py:204
  268.6 0.6 multiply_reduce_fusion
  269.2 1.0 reshape.86
  270.2 0.1 reshape.87
  270.3 0.6 copy.43
  (5 shorter events, 0.1 us)
Async XLA Ops:
  7.2 230.2 %reduce-scatter.4.cloned.1.call-start = ((), (), s32[]{:S(2)}) async-start(), calls=%async_computation.2 | async-start | bytes 5242880
  168.4 7.5 %copy-start.2 = (bf16[1,1024,1792]{2,1,0:T(8,128)(2,1)S(1)}, bf16[1,1024,1792]{2,1,0:T(8,128)(2,1)}, u32[]{:S(2)}) copy-start(bf16[1,1024,1792]{2,1,0:T(8,128)(2,1)} %param.9) | copy-start | bytes 11010052
  175.9 9.5 %copy-start = (bf16[32,64,1792]{2,1,0:T(8,128)(2,1)}, bf16[32,64,1792]{2,1,0:T(8,128)(2,1)S(1)}, u32[]{:S(2)}) copy-start(bf16[32,64,1792]{2,1,0:T(8,128)(2,1)S(1)} %convolution_convert_fusion) | copy-start | bytes 22020100
  237.4 31.2 %all-to-all-start = ((bf16[8,64,1024]{2,1,0:T(8,128)(2,1)}), bf16[8,64,1024]{2,1,0:T(8,128)(2,1)S(1)}, u32[]{:S(2)}, u32[]{:S(2)}) async-start(bf16[8,64,1024]{2,1,0:T(8,128)(2,1)} %bitcast.45), calls=%async_computation | async-start | bytes 2097152 | tf_op jit(solution)/shard_map/all_to_all | solution.py:204
  242.0 5.2 %copy-start.1 = (bf16[128,2,1024]{2,1,0:T(2,128)(2,1)S(1)}, bf16[128,2,1024]{2,1,0:T(2,128)(2,1)}, u32[]{:S(2)}) copy-start(bf16[128,2,1024]{2,1,0:T(2,128)(2,1)} %param.5) | copy-start | bytes 1572868
Sparse Core Ops, SparseCore 0:
  185.5 51.8 reduce-scatter.3

commit v3 on v2

--- a/solution.py
+++ b/solution.py
@@ -33,15 +33,15 @@
 
     def to_group(step):
         there = other(group, step, groups)
-        return remote(quarters.at[there], every.at[group, mine], dp_send.at[step], dp_recv.at[step], (there, mine))
+        return remote(quarters.at[there], every.at[mine, group], dp_send.at[step], dp_recv.at[step], (there, mine))
 
     def to_expert(step):
         there = other(mine, step, columns)
-        return remote(packed.at[there], rows.at[group, mine], rows_send.at[step], rows_recv.at[step], (group, there))
+        return remote(packed.at[there], rows.at[mine, group], rows_send.at[step], rows_recv.at[step], (group, there))
 
     def chunk(start, step):
         source = lax.rem(group - step + groups, groups)
-        place = every.at[source, start * 2 + core]
+        place = every.at[start * 2 + core, source]
         return place, source
 
     def on_line(start, step, move, first=False):
@@ -57,12 +57,12 @@
 
     def pass_on(step, hop):
         start = lax.rem(mine - step + columns, columns)
-        place = rows.at[group, start]
+        place = rows.at[start, group]
         origin = packed.at[mine] if step == 0 else place
         return remote(origin, place, pass_send.at[hop, step], pass_recv.at[hop, step], (other(group, hop, groups), mine))
 
-    own_cot = pltpu.make_async_copy(quarters.at[group], every.at[group, mine], local_sem.at[0])
-    own_rows = pltpu.make_async_copy(packed.at[mine], rows.at[group, mine], local_sem.at[1])
+    own_cot = pltpu.make_async_copy(quarters.at[group], every.at[mine, group], local_sem.at[0])
+    own_rows = pltpu.make_async_copy(packed.at[mine], rows.at[mine, group], local_sem.at[1])
 
     for step in range(1, groups):
         to_group(step).start()
@@ -132,6 +132,92 @@
             pass_on(peer, hop).wait()
 
 
+def product(groups, columns, cot, matrix, sent, grad, back, partial, arrived, total,
+            part_send, part_recv, back_send, back_recv):
+    group, mine = lax.axis_index("dp"), lax.axis_index("expert")
+    capacity, width = total.shape[1:]
+    part = cot.shape[-1]
+
+    barrier = pltpu.get_barrier_semaphore()
+    for step in range(1, groups):
+        pl.semaphore_signal(barrier, inc=1, device_id=(lax.rem(group + step, groups), mine), device_id_type=MESH)
+    for step in range(1, columns):
+        pl.semaphore_signal(barrier, inc=1, device_id=(group, lax.rem(mine + step, columns)), device_id_type=MESH)
+    pl.semaphore_wait(barrier, groups + columns - 2)
+
+    def to_group(turn, step):
+        there = lax.rem(group + step, groups)
+        return pltpu.make_async_remote_copy(
+            src_ref=partial.at[turn, there],
+            dst_ref=arrived.at[step, turn],
+            send_sem=part_send.at[step, turn],
+            recv_sem=part_recv.at[step, turn],
+            device_id=(there, mine),
+            device_id_type=MESH,
+        )
+
+    def to_expert(turn):
+        return pltpu.make_async_remote_copy(
+            src_ref=total.at[turn],
+            dst_ref=back.at[mine],
+            send_sem=back_send.at[turn],
+            recv_sem=back_recv.at[turn],
+            device_id=(group, lax.rem(mine + turn + 1, columns)),
+            device_id_type=MESH,
+        )
+
+    def multiply(turn, carry):
+        there = lax.rem(mine + turn + 1, columns)
+        block = cot[there].reshape(groups * capacity, part)
+        terms = lax.dot_general(block, matrix[...], (((1,), (1,)), ((), ())), preferred_element_type=jnp.float32)
+        partial[turn] = terms.astype(jnp.bfloat16).reshape(groups, capacity, width)
+        for step in range(1, groups):
+            to_group(turn, step).start()
+        return carry
+
+    lax.fori_loop(0, columns, multiply, 0)
+
+    span = 256
+    slots = columns * groups * capacity
+
+    def outer(tile, carry):
+        at = pl.ds(pl.multiple_of(tile * span, span), span)
+        block = cot[:, :, :, at].reshape(slots, span)
+        grad[:, at] = jnp.dot(sent[...], block, preferred_element_type=jnp.float32).astype(jnp.bfloat16)
+        return carry
+
+    lax.fori_loop(0, part // span, outer, 0)
+
+    def add(turn):
+        for step in range(1, groups):
+            to_group(turn, step).wait_recv()
+        value = partial[turn, group].astype(jnp.float32)
+        for step in range(1, groups):
+            value = value + arrived[step, turn].astype(jnp.float32)
+        return value.astype(jnp.bfloat16)
+
+    def hand_back(turn, carry):
+        total[turn] = add(turn)
+        to_expert(turn).start()
+        return carry
+
+    lax.fori_loop(0, columns - 1, hand_back, 0)
+    back[mine] = add(columns - 1)
+
+    def finish(turn, carry):
+        for step in range(1, groups):
+            to_group(turn, step).wait_send()
+        return carry
+
+    lax.fori_loop(0, columns, finish, 0)
+
+    def arrive(turn, carry):
+        to_expert(turn).wait()
+        return carry
+
+    lax.fori_loop(0, columns - 1, arrive, 0)
+
+
 def gathered(hidden, routes, gates, cotangent, weight):
     tokens, top, width = hidden.shape
     columns, groups = lax.axis_size("expert"), lax.axis_size("dp")
@@ -162,8 +248,8 @@
     every, rows = pl.pallas_call(
         functools.partial(exchange, groups, columns),
         out_shape=(
-            jax.ShapeDtypeStruct((groups, columns, tokens, part), jnp.bfloat16),
-            jax.ShapeDtypeStruct((groups, columns, capacity, width + tokens), jnp.bfloat16),
+            jax.ShapeDtypeStruct((columns, groups, tokens, part), jnp.bfloat16),
+            jax.ShapeDtypeStruct((columns, groups, capacity, width + tokens), jnp.bfloat16),
         ),
         in_specs=[pl.BlockSpec(memory_space=pl.ANY)] * 2,
         out_specs=[pl.BlockSpec(memory_space=pl.ANY)] * 2,
@@ -186,22 +272,36 @@
     )(quarters, packed)
 
     blocks = groups * columns
-    sent, token_of = rows[..., :width], rows[..., width:]
+    token_of = rows[..., width:]
     cot = lax.dot_general(
         token_of.reshape(blocks, capacity, tokens),
         every.reshape(blocks, tokens, part),
         (((2,), (1,)), ((0,), (0,))),
         preferred_element_type=jnp.float32,
-    ).astype(jnp.bfloat16).reshape(blocks * capacity, part)
-    partial_back = lax.dot_general(
-        cot, weight[0], (((1,), (1,)), ((), ())), preferred_element_type=jnp.float32
-    ).astype(jnp.bfloat16)
-    partial_back = partial_back.reshape(groups, columns, capacity, width)
-    summed = lax.psum_scatter(partial_back, "dp", scatter_dimension=0, tiled=True)
-    grad_matrix = lax.dot_general(
-        sent.reshape(blocks * capacity, width), cot, (((0,), (0,)), ((), ())), preferred_element_type=jnp.float32
-    )
-    returned = lax.all_to_all(summed[0], "expert", split_axis=0, concat_axis=0, tiled=True)
+    ).astype(jnp.bfloat16).reshape(columns, groups, capacity, part)
+    sent = rows[..., :width].reshape(blocks * capacity, width).T
+    grad_matrix, returned = pl.pallas_call(
+        functools.partial(product, groups, columns),
+        out_shape=(
+            jax.ShapeDtypeStruct((width, part), jnp.bfloat16),
+            jax.ShapeDtypeStruct((columns, capacity, width), jnp.bfloat16),
+        ),
+        in_specs=[pl.BlockSpec(memory_space=pltpu.VMEM)] * 3,
+        out_specs=[pl.BlockSpec(memory_space=pltpu.VMEM)] * 2,
+        scratch_shapes=[
+            pltpu.VMEM((columns, groups, capacity, width), jnp.bfloat16),
+            pltpu.VMEM((groups, columns, capacity, width), jnp.bfloat16),
+            pltpu.VMEM((columns, capacity, width), jnp.bfloat16),
+            sems((groups, columns)),
+            sems((groups, columns)),
+            sems((columns,)),
+            sems((columns,)),
+        ],
+        compiler_params=pltpu.CompilerParams(
+            collective_id=1, has_side_effects=True, vmem_limit_bytes=56 << 20
+        ),
+        name="product",
+    )(cot, weight[0], sent)
     back = lax.dot_general(
         choose, returned.reshape(columns * capacity, width), (((0,), (0,)), ((), ())), preferred_element_type=jnp.float32
     )
@@ -211,7 +311,7 @@
     grad_gates = jnp.sum(
         hidden.reshape(slots, width).astype(jnp.float32) * back, axis=1
     ).reshape(tokens, top)
-    return (grad_hidden, grad_gates, grad_matrix.astype(jnp.bfloat16)[None])
+    return (grad_hidden, grad_gates, grad_matrix[None])
 
 
 def dispatched(hidden, routes, gates, cotangent, weight):

time: 278 us -> 249 us (0.90)
  waiting for transfers between devices: 60.2 us -> 0 us
  Pallas kernels: 147 us -> 206 us
  matrix products: 31 us -> 12.7 us
  between operations: 14.2 us -> 0.76 us
  local copies, waits for them, and re-layouts: 16.4 us -> 24.7 us
  starting transfers between devices: 4.65 us -> 0 us
    pallas_call x0 -> x1, Pallas kernels: none -> 58.9 us  [gathered(): pl.pallas_call(functools.partial(product, groups, columns), out_shape=(ja...]
    unnamed x2 -> x0, waiting for transfers between devices: 52 us -> none
    dot_general x2 -> x0, matrix products: 22.5 us -> none  [the longest x1 13.1 us: gathered(): lax.dot_general(sent.reshape(blocks * capacity, width), cot, (((0,), (0,)...]
    all_to_all x1 -> x0, waiting for transfers between devices: 8.19 us -> none  [gathered(): lax.all_to_all(summed[0], 'expert', split_axis=0, concat_axis=0, tiled=True)]
    reshape x0 -> x1, local copies, waits for them, and re-layouts: none -> 6.49 us  [gathered(): sent = rows[..., :width].reshape(blocks * capacity, width).T]
    all_to_all x1 -> x0, starting transfers between devices: 4.61 us -> none  [gathered(): lax.all_to_all(summed[0], 'expert', split_axis=0, concat_axis=0, tiled=True)]
    unnamed x10 -> x11, local copies, waits for them, and re-layouts: 5.52 us -> 9.62 us
    dot_general x1, matrix products: 7.45 us -> 10.4 us  [gathered(): lax.dot_general(token_of.reshape(blocks, capacity, tokens), every.reshape...]
  transfers between devices with their start and end apart: 2 -> 0, of which waited for: 2 -> 0; matrix products, arithmetic and copies ran while one was open for 7% -> 0% of each run, Pallas kernels for 0% -> 0%
where the time goes in v3:
time: 249 us; the launch traced here: 248 us
  Pallas kernels  206 us (83%)
  local copies, waits for them, and re-layouts  24.7 us (10%)
  matrix products  12.7 us (5%)
  other arithmetic  4.15 us (2%)
    pallas_call x1, Pallas kernels, gathered(): pl.pallas_call(functools.partial(exchange, groups, columns), out_shape=(j...  147 us
    pallas_call x1, Pallas kernels, gathered(): pl.pallas_call(functools.partial(product, groups, columns), out_shape=(ja...  58.9 us
    dot_general x1, matrix products, gathered(): lax.dot_general(token_of.reshape(blocks, capacity, tokens), every.reshape...  10.4 us
    unnamed x11, local copies, waits for them, and re-layouts  9.62 us
    reshape x1, local copies, waits for them, and re-layouts, gathered(): sent = rows[..., :width].reshape(blocks * capacity, width).T  6.49 us

profile of v3, /device:TPU:0, one launch (start us, length us, event | category | flops | bytes accessed | tf_op | source)
XLA Modules:
  0.0 248.4 jit_solution(6537026978939545717)
XLA Ops:
  0.6 0.8 copy.31
  1.4 0.1 eq.70
  1.6 0.6 reduce-window.6
  2.2 0.2 slice_reduce_fusion
  2.4 0.1 reshape.73
  2.6 0.1 fusion.7
  2.6 0.1 reduce_sum.21
  2.8 0.1 copy.36
  2.9 0.7 multiply_add_fusion
  3.6 0.1 fusion.5
  3.7 0.8 copy.30
  4.4 1.5 multiply_convert_fusion.1
  6.0 0.2 reshape.76
  6.2 0.4 convolution_convert_fusion.1
  6.6 1.1 pad_maximum_fusion
  7.8 3.3 %copy.33 = bf16[128,7168]{0,1:T(8,128)(2,1)S(1)} copy(bf16[128,7168]{1,0:T(8,128)(2,1)} %param.8) | data formatting | bytes 3670016 | tf_op args[3]
  11.1 2.4 copy.34
  13.5 147.3 %exchange.1 = (bf16[8,4,128,1792]{3,2,1,0:T(8,128)(2,1)}, bf16[8,4,64,1152]{3,2,1,0:T(8,128)(2,1)}) custom-call(bf16[4,128,1792]{2,1,0:T(8,128)(2,1)} %bitcast.32, bf16[8,64,1152]{2,1,0:T(8,128)(2,1)} %bitcast.35), custom_call_target="tpu_custom_call" | custom-call | tf_op jit(solution)/shard_map/exchange/pallas_call | solution.py:248
  160.8 0.0 slice-start
  160.8 1.2 slice.22
  162.0 0.0 slice-start.1
  162.0 10.4 %convolution_convert_fusion = bf16[32,64,1792]{2,1,0:T(8,128)(2,1)} fusion(bf16[32,64,128]{2,1,0:T(8,128)(2,1)S(1)} %bitcast.36, bf16[32,128,1792]{2,1,0:T(8,128)(2,1)} %bitcast.28), kind=kOutput, calls=%fused_computation | convolution fusion | flops 943194112 | bytes 22544384 | tf_op jit(solution)/shard_map/dot_general | solution.py:276
  172.5 0.0 slice-done
  172.5 0.0 slice-done.1
  172.5 2.6 %slice.23 = bf16[8,4,64,1024]{3,2,1,0:T(8,128)(2,1)} slice(bf16[8,4,64,1152]{3,2,1,0:T(8,128)(2,1)S(1)} %bitcast.34), slice={[0:8], [0:4], [0:64], [0:1024]} | slice | bytes 8388608 | tf_op jit(solution)/shard_map/slice | solution.py:282
  175.1 6.5 %copy.37 = bf16[2048,1024]{0,1:T(8,128)(2,1)} copy(bf16[2048,1024]{1,0:T(8,128)(2,1)} %bitcast.29) | data formatting | bytes 8388608 | tf_op jit(solution)/shard_map/reshape | solution.py:282
  181.6 0.0 copy-start
  181.6 58.9 %product.1 = (bf16[1024,1792]{1,0:T(8,128)(2,1)}, bf16[8,64,1024]{2,1,0:T(8,128)(2,1)}) custom-call(bf16[8,4,64,1792]{3,2,1,0:T(8,128)(2,1)} %bitcast.27, bf16[1024,1792]{1,0:T(8,128)(2,1)} %bitcast.38, bf16[1024,2048]{1,0:T(8,128)(2,1)} %bitcast.30), custom_call_target="tpu_custom_call" | custom-call | tf_op jit(solution)/shard_map/product/pallas_call | solution.py:283
  240.5 0.1 mul.39
  240.6 0.0 copy-done
  240.6 0.1 reshape.85
  240.8 1.8 multiply_reduce_fusion
  242.6 1.0 reshape.83
  243.6 0.1 reshape.84
  243.7 0.6 copy.38
  244.3 4.1 %copy.40 = bf16[1,1024,1792]{2,1,0:T(8,128)(2,1)} copy(bf16[1,1024,1792]{2,1,0:T(8,128)(2,1)} %bitcast.37) | data formatting | bytes 7340032
  (6 shorter events, 0.1 us)
Async XLA Ops:
  160.8 11.7 %slice-start = ((s8[4718592]{0:T(1024)(128)(4,1)}), s8[4194304]{0:T(1024)(128)(4,1)S(1)}, s32[]{:S(2)}) async-start(s8[4718592]{0:T(1024)(128)(4,1)} %bitcast.33), calls=%async_computation | async-start | bytes 8388608
  162.0 10.4 %slice-start.1 = ((s8[4718592]{0:T(1024)(128)(4,1)}), s8[524288]{0:T(1024)(128)(4,1)S(1)}, s32[]{:S(2)}) async-start(s8[4718592]{0:T(1024)(128)(4,1)} %bitcast.33), calls=%async_computation.1 | async-start | bytes 1048576
  181.6 59.0 %copy-start = (bf16[128,2,1024]{2,1,0:T(2,128)(2,1)S(1)}, bf16[128,2,1024]{2,1,0:T(2,128)(2,1)}, u32[]{:S(2)}) copy-start(bf16[128,2,1024]{2,1,0:T(2,128)(2,1)} %param.5) | copy-start | bytes 1572868

commit v4 on v3

--- a/solution.py
+++ b/solution.py
@@ -132,12 +132,17 @@
             pass_on(peer, hop).wait()
 
 
-def product(groups, columns, cot, matrix, sent, grad, back, partial, arrived, total,
-            part_send, part_recv, back_send, back_recv):
+def product(groups, columns, every, matrix, rows, grad, back, cot, sent, chunk, partial, arrived, total,
+            part_send, part_recv, back_send, back_recv, chunk_sem):
     group, mine = lax.axis_index("dp"), lax.axis_index("expert")
     capacity, width = total.shape[1:]
     part = cot.shape[-1]
 
+    def fetch(turn):
+        there, slot = lax.rem(mine + turn + 1, columns), lax.rem(turn, 2)
+        return pltpu.make_async_copy(every.at[there], chunk.at[slot], chunk_sem.at[slot])
+
+    fetch(0).start()
     barrier = pltpu.get_barrier_semaphore()
     for step in range(1, groups):
         pl.semaphore_signal(barrier, inc=1, device_id=(lax.rem(group + step, groups), mine), device_id_type=MESH)
@@ -168,6 +173,16 @@
 
     def multiply(turn, carry):
         there = lax.rem(mine + turn + 1, columns)
+        slot = lax.rem(turn, 2)
+
+        @pl.when(turn + 1 < columns)
+        def _():
+            fetch(turn + 1).start()
+
+        fetch(turn).wait()
+        for source in range(groups):
+            picked = jnp.dot(rows[there, source, :, width:], chunk[slot, source], preferred_element_type=jnp.float32)
+            cot[there, source] = picked.astype(jnp.bfloat16)
         block = cot[there].reshape(groups * capacity, part)
         terms = lax.dot_general(block, matrix[...], (((1,), (1,)), ((), ())), preferred_element_type=jnp.float32)
         partial[turn] = terms.astype(jnp.bfloat16).reshape(groups, capacity, width)
@@ -176,6 +191,10 @@
         return carry
 
     lax.fori_loop(0, columns, multiply, 0)
+
+    for start in range(columns):
+        at = pl.ds(start * groups * capacity, groups * capacity)
+        sent[:, at] = rows[start, :, :, :width].reshape(groups * capacity, width).T
 
     span = 256
     slots = columns * groups * capacity
@@ -271,24 +290,18 @@
         name="exchange",
     )(quarters, packed)
 
-    blocks = groups * columns
-    token_of = rows[..., width:]
-    cot = lax.dot_general(
-        token_of.reshape(blocks, capacity, tokens),
-        every.reshape(blocks, tokens, part),
-        (((2,), (1,)), ((0,), (0,))),
-        preferred_element_type=jnp.float32,
-    ).astype(jnp.bfloat16).reshape(columns, groups, capacity, part)
-    sent = rows[..., :width].reshape(blocks * capacity, width).T
     grad_matrix, returned = pl.pallas_call(
         functools.partial(product, groups, columns),
         out_shape=(
             jax.ShapeDtypeStruct((width, part), jnp.bfloat16),
             jax.ShapeDtypeStruct((columns, capacity, width), jnp.bfloat16),
         ),
-        in_specs=[pl.BlockSpec(memory_space=pltpu.VMEM)] * 3,
+        in_specs=[pl.BlockSpec(memory_space=pl.ANY)] + [pl.BlockSpec(memory_space=pltpu.VMEM)] * 2,
         out_specs=[pl.BlockSpec(memory_space=pltpu.VMEM)] * 2,
         scratch_shapes=[
+            pltpu.VMEM((columns, groups, capacity, part), jnp.bfloat16),
+            pltpu.VMEM((width, columns * groups * capacity), jnp.bfloat16),
+            pltpu.VMEM((2, groups, tokens, part), jnp.bfloat16),
             pltpu.VMEM((columns, groups, capacity, width), jnp.bfloat16),
             pltpu.VMEM((groups, columns, capacity, width), jnp.bfloat16),
             pltpu.VMEM((columns, capacity, width), jnp.bfloat16),
@@ -296,12 +309,13 @@
             sems((groups, columns)),
             sems((columns,)),
             sems((columns,)),
+            sems((2,)),
         ],
         compiler_params=pltpu.CompilerParams(
             collective_id=1, has_side_effects=True, vmem_limit_bytes=56 << 20
         ),
         name="product",
-    )(cot, weight[0], sent)
+    )(every, weight[0], rows)
     back = lax.dot_general(
         choose, returned.reshape(columns * capacity, width), (((0,), (0,)), ((), ())), preferred_element_type=jnp.float32
     )

time: 249 us -> 227 us (0.912)
  matrix products: 12.7 us -> 2.25 us
  local copies, waits for them, and re-layouts: 24.7 us -> 14.4 us
    dot_general x1 -> x0, matrix products: 10.4 us -> none  [gathered(): lax.dot_general(token_of.reshape(blocks, capacity, tokens), every.reshape...]
    reshape x1 -> x0, local copies, waits for them, and re-layouts: 6.49 us -> none  [gathered(): sent = rows[..., :width].reshape(blocks * capacity, width).T]
    slice x3 -> x1, local copies, waits for them, and re-layouts: 4.04 us -> 0.21 us  [the longest x1 2.59 us: gathered(): sent = rows[..., :width].reshape(blocks * capacity, width).T]
    unnamed x11 -> x7, local copies, waits for them, and re-layouts: 9.62 us -> 9.61 us
where the time goes in v4:
time: 227 us; the launch traced here: 226 us
  Pallas kernels  205 us (90%)
  local copies, waits for them, and re-layouts  14.4 us (6%)
  other arithmetic  4.15 us (2%)
    pallas_call x1, Pallas kernels, gathered(): pl.pallas_call(functools.partial(exchange, groups, columns), out_shape=(j...  147 us
    pallas_call x1, Pallas kernels, gathered(): pl.pallas_call(functools.partial(product, groups, columns), out_shape=(ja...  57.6 us
    unnamed x7, local copies, waits for them, and re-layouts  9.61 us

profile of v4, /device:TPU:0, one launch (start us, length us, event | category | flops | bytes accessed | tf_op | source)
XLA Modules:
  0.0 226.3 jit_solution(18119768634609127864)
XLA Ops:
  0.6 0.8 copy.28
  1.4 0.1 eq.70
  1.6 0.6 reduce-window.6
  2.2 0.2 slice_reduce_fusion
  2.4 0.1 reshape.61
  2.6 0.1 fusion.7
  2.6 0.1 reduce_sum.21
  2.8 0.1 copy.33
  2.9 0.7 multiply_add_fusion
  3.6 0.1 fusion.5
  3.7 0.8 copy.27
  4.4 1.5 multiply_convert_fusion.1
  6.0 0.2 reshape.64
  6.2 0.4 convolution_convert_fusion
  6.6 1.1 pad_maximum_fusion
  7.8 3.3 %copy.30 = bf16[128,7168]{0,1:T(8,128)(2,1)S(1)} copy(bf16[128,7168]{1,0:T(8,128)(2,1)} %param.8) | data formatting | bytes 3670016 | tf_op args[3]
  11.1 2.4 %copy.31 = bf16[128,4,1792]{2,0,1:T(8,128)(2,1)} copy(bf16[128,4,1792]{0,2,1:T(8,128)(2,1)S(1)} %bitcast.20) | data formatting | bytes 3670016 | tf_op jit(solution)/shard_map/reshape | solution.py:246
  13.5 147.3 %exchange.1 = (bf16[8,4,128,1792]{3,2,1,0:T(8,128)(2,1)}, bf16[8,4,64,1152]{3,2,1,0:T(8,128)(2,1)}) custom-call(bf16[4,128,1792]{2,1,0:T(8,128)(2,1)} %bitcast.21, bf16[8,64,1152]{2,1,0:T(8,128)(2,1)} %bitcast.22), custom_call_target="tpu_custom_call" | custom-call | tf_op jit(solution)/shard_map/exchange/pallas_call | solution.py:267
  160.8 0.0 copy-start
  160.8 57.6 %product.1 = (bf16[1024,1792]{1,0:T(8,128)(2,1)}, bf16[8,64,1024]{2,1,0:T(8,128)(2,1)}) custom-call(bf16[8,4,128,1792]{3,2,1,0:T(8,128)(2,1)} %get-tuple-element.7.every, bf16[1024,1792]{1,0:T(8,128)(2,1)} %bitcast.24, bf16[8,4,64,1152]{3,2,1,0:T(8,128)(2,1)} %get-tuple-element.8.rows), custom_call_target="tpu_custom_call" | custom-call | tf_op jit(solution)/shard_map/product/pallas_call | solution.py:293
  218.3 0.1 mul.39
  218.5 0.0 copy-done
  218.5 0.1 reshape.69
  218.7 1.8 multiply_reduce_fusion
  220.4 1.0 reshape.67
  221.4 0.1 reshape.68
  221.6 0.6 copy.34
  222.2 4.1 %copy.36 = bf16[1,1024,1792]{2,1,0:T(8,128)(2,1)} copy(bf16[1,1024,1792]{2,1,0:T(8,128)(2,1)} %bitcast.23) | data formatting | bytes 7340032
  (5 shorter events, 0.1 us)
Async XLA Ops:
  160.8 57.7 %copy-start = (bf16[128,2,1024]{2,1,0:T(2,128)(2,1)S(1)}, bf16[128,2,1024]{2,1,0:T(2,128)(2,1)}, u32[]{:S(2)}) copy-start(bf16[128,2,1024]{2,1,0:T(2,128)(2,1)} %param.5) | copy-start | bytes 1572868

commit v5 on v4

--- a/solution.py
+++ b/solution.py
@@ -10,11 +10,16 @@
 MESH = pl.DeviceIdType.MESH
 
 
-def exchange(groups, columns, quarters, packed, every, rows, local_sem, dp_send, dp_recv, side_send,
+def exchange(groups, columns, cotangent, packed, every, rows, local_sem, dp_send, dp_recv, side_send,
              up_send, down_send, line_recv, side_recv, rows_send, rows_recv, pass_send, pass_recv):
     group, mine = lax.axis_index("dp"), lax.axis_index("expert")
     depth = columns // 2
     level, core = mine // 2, lax.rem(mine, 2)
+
+    part = cotangent.shape[1] // groups
+
+    def quarter(index):
+        return cotangent.at[:, pl.ds(pl.multiple_of(index * part, part), part)]
 
     def other(index, step, size):
         return lax.rem(index + step, size)
@@ -33,7 +38,7 @@
 
     def to_group(step):
         there = other(group, step, groups)
-        return remote(quarters.at[there], every.at[mine, group], dp_send.at[step], dp_recv.at[step], (there, mine))
+        return remote(quarter(there), every.at[mine, group], dp_send.at[step], dp_recv.at[step], (there, mine))
 
     def to_expert(step):
         there = other(mine, step, columns)
@@ -47,12 +52,12 @@
     def on_line(start, step, move, first=False):
         place, source = chunk(start, step)
         send = (up_send if move > 0 else down_send).at[start, step]
-        origin = quarters.at[group] if first else place
+        origin = quarter(group) if first else place
         return remote(origin, place, send, line_recv.at[start, step], (group, (level + move) * 2 + core))
 
     def to_side(start, step, first=False):
         place, source = chunk(start, step)
-        origin = quarters.at[group] if first else place
+        origin = quarter(group) if first else place
         return remote(origin, place, side_send.at[start, step], side_recv.at[start, step], (group, level * 2 + 1 - core))
 
     def pass_on(step, hop):
@@ -61,7 +66,7 @@
         origin = packed.at[mine] if step == 0 else place
         return remote(origin, place, pass_send.at[hop, step], pass_recv.at[hop, step], (other(group, hop, groups), mine))
 
-    own_cot = pltpu.make_async_copy(quarters.at[group], every.at[mine, group], local_sem.at[0])
+    own_cot = pltpu.make_async_copy(quarter(group), every.at[mine, group], local_sem.at[0])
     own_rows = pltpu.make_async_copy(packed.at[mine], rows.at[mine, group], local_sem.at[1])
 
     for step in range(1, groups):
@@ -243,7 +248,6 @@
     capacity = min(tokens, 2 * tokens * top // columns)
     slots = tokens * top
     part = cotangent.shape[1] // groups
-    quarters = cotangent.reshape(tokens, groups, part).transpose(1, 0, 2)
 
     flat = routes.reshape(slots)
     named = (flat[:, None] == jnp.arange(columns, dtype=jnp.int32)[None, :]).astype(jnp.int32)
@@ -288,7 +292,7 @@
         ],
         compiler_params=pltpu.CompilerParams(collective_id=0, has_side_effects=True),
         name="exchange",
-    )(quarters, packed)
+    )(cotangent, packed)
 
     grad_matrix, returned = pl.pallas_call(
         functools.partial(product, groups, columns),

time: 227 us -> 221 us (0.974)
  local copies, waits for them, and re-layouts: 14.4 us -> 8.65 us
    unnamed x7 -> x6, local copies, waits for them, and re-layouts: 9.61 us -> 6.33 us
    reshape x1 -> x0, local copies, waits for them, and re-layouts: 2.43 us -> none  [gathered(): quarters = cotangent.reshape(tokens, groups, part).transpose(1, 0, 2)]
where the time goes in v5:
time: 221 us
  Pallas kernels  205 us (93%)
  local copies, waits for them, and re-layouts  8.65 us (4%)
  other arithmetic  4.13 us (2%)
  matrix products  2.25 us (1%)
    pallas_call x1, Pallas kernels, gathered(): pl.pallas_call(functools.partial(exchange, groups, columns), out_shape=(j...  147 us
    pallas_call x1, Pallas kernels, gathered(): pl.pallas_call(functools.partial(product, groups, columns), out_shape=(ja...  57.6 us
    unnamed x6, local copies, waits for them, and re-layouts  6.33 us

profile of v5, /device:TPU:0, one launch (start us, length us, event | category | flops | bytes accessed | tf_op | source)
XLA Modules:
  0.0 220.6 jit_solution(4684132416740958986)
XLA Ops:
  0.6 0.8 copy.24
  1.4 0.1 eq.70
  1.6 0.6 reduce-window.6
  2.2 0.2 slice_reduce_fusion
  2.4 0.1 reshape.58
  2.6 0.1 fusion.7
  2.6 0.1 reduce_sum.21
  2.8 0.1 copy.27
  2.9 0.7 multiply_add_fusion
  3.6 0.1 fusion.5
  3.7 0.8 copy.23
  4.4 1.5 multiply_convert_fusion.1
  6.0 0.2 reshape.60
  6.2 0.4 convolution_convert_fusion
  6.6 1.1 pad_maximum_fusion
  7.7 147.3 %exchange.1 = (bf16[8,4,128,1792]{3,2,1,0:T(8,128)(2,1)}, bf16[8,4,64,1152]{3,2,1,0:T(8,128)(2,1)}) custom-call(bf16[128,7168]{1,0:T(8,128)(2,1)} %cotangent.1, bf16[8,64,1152]{2,1,0:T(8,128)(2,1)} %bitcast.18), custom_call_target="tpu_custom_call" | custom-call | tf_op jit(solution)/shard_map/exchange/pallas_call | solution.py:271
  155.0 0.0 copy-start
  155.0 57.6 %product.1 = (bf16[1024,1792]{1,0:T(8,128)(2,1)}, bf16[8,64,1024]{2,1,0:T(8,128)(2,1)}) custom-call(bf16[8,4,128,1792]{3,2,1,0:T(8,128)(2,1)} %get-tuple-element.7.every, bf16[1024,1792]{1,0:T(8,128)(2,1)} %bitcast.20, bf16[8,4,64,1152]{3,2,1,0:T(8,128)(2,1)} %get-tuple-element.8.rows), custom_call_target="tpu_custom_call" | custom-call | tf_op jit(solution)/shard_map/product/pallas_call | solution.py:297
  212.6 0.1 mul.39
  212.7 0.0 copy-done
  212.7 0.1 reshape.65
  212.9 1.8 multiply_reduce_fusion
  214.7 1.0 reshape.63
  215.7 0.1 reshape.64
  215.8 0.6 copy.28
  216.5 4.1 %copy.30 = bf16[1,1024,1792]{2,1,0:T(8,128)(2,1)} copy(bf16[1,1024,1792]{2,1,0:T(8,128)(2,1)} %bitcast.19) | data formatting | bytes 7340032
  (5 shorter events, 0.1 us)
Async XLA Ops:
  155.0 57.7 %copy-start = (bf16[128,2,1024]{2,1,0:T(2,128)(2,1)S(1)}, bf16[128,2,1024]{2,1,0:T(2,128)(2,1)}, u32[]{:S(2)}) copy-start(bf16[128,2,1024]{2,1,0:T(2,128)(2,1)} %param.5) | copy-start | bytes 1572868
